TPU v7x, 32 devices: a whole 2x2x4 slice. The times are simulated.
32 devices in a mesh: tm: 16 (over z, x, core), panel: 2 (over y).
Axes of the slice: x: 2, y: 2, z: 4, core: 2. Of those that a mesh axis runs over, the one named last changes fastest.
Arguments:
- transition: bfloat16 [16, 1024, 1024], P('tm', None, 'panel'), may hold values from -1 to 1
- drift: bfloat16 [16, 1024], P('tm'), may hold values from -6 to 6
- spread: bfloat16 [16, 1024, 1024], P('tm', None, 'panel'), may hold values from -1 to 1, as said below
- belief: bfloat16 [16, 1024], P('tm'), may hold values from -6 to 6
- precision: bfloat16 [16, 1024, 1024], P('tm', None, 'panel'), may hold values from -1 to 1, as said below
- probe_hosts: int32 [16, 256], P('tm'), may hold values from 0 to 511
- probe_values: float32 [16, 256], P('tm'), may hold values from -6 to 6
Outputs:
- sum_transition: bfloat16 [16, 1024, 1024], P('tm', None, 'panel')
- sum_drift: bfloat16 [16, 1024], P('tm')
- sum_spread: bfloat16 [16, 1024, 1024], P('tm', None, 'panel')
- sum_belief: bfloat16 [16, 1024], P('tm')
- sum_precision: bfloat16 [16, 1024, 1024], P('tm', None, 'panel')
Inputs may be any that keep to these rules, and one draw needn't show every extreme that they name: `spread`: every 1024 x 1024 block is symmetric. `precision`: every 1024 x 1024 block is symmetric.
All inputs are finite; a program needn't handle non-finite values.
Results may differ from a plain program's by a relative error of at most 0.012.
The roundings to bfloat16 on the way count: a program that leaves them out, or rounds other values in their place, can miss the bound.
Values may be sent and summed in bfloat16 or wider, within the bound.
A program may use at most 64 MiB of HBM per device.

v0:
```python
import functools

import jax
import jax.numpy as jnp
from jax import lax
from jax.experimental import pallas as pl
from jax.experimental.pallas import tpu as pltpu
from jax.sharding import PartitionSpec as P

NS = 2
TERMS = 2**NS - 1
F32 = jnp.float32
BF16 = jnp.bfloat16
MESH = pl.DeviceIdType.MESH
NN = (((1,), (0,)), ((), ()))
NT = (((1,), (1,)), ((), ()))
TN = (((0,), (0,)), ((), ()))


def dot(lhs, rhs, dims=NN):
    return lax.dot_general(lhs, rhs, dims, preferred_element_type=F32)


def kernel(
    panels, names,
    a_ref, c_ref, j_ref, b_ref, eta_ref, hosts_ref, values_ref,
    a_out, c_out, j_out, vec_out,
    s0, a0, s1, a1, v0, v1, anchor, cur, inner, weighted, send_sem, recv_sem,
):
    states, width = a_ref.shape
    tile = min(width, 256)
    tiles = width // tile
    time = lax.axis_index("tm")
    me = lax.axis_index("panel")
    core = lax.rem(time, 2)
    half = lax.rem(lax.div(time, 2), 2)
    core_peer = time + 1 - 2 * core
    side_peer = time + 2 - 4 * half
    cross_peer = core_peer + 2 - 4 * half
    own_cols = pl.ds(pl.multiple_of(me * width, width), width)

    def sem(name):
        return names.setdefault(name, len(names))

    def copy(name, src, dst, at, panel=None):
        index = sem(name)
        return pltpu.make_async_remote_copy(
            src_ref=src, dst_ref=dst,
            send_sem=send_sem.at[index], recv_sem=recv_sem.at[index],
            device_id=(at, me if panel is None else panel), device_id_type=MESH,
        )

    def panel_block(ref, slot, rows, cols):
        return ref.at[slot, rows, cols]

    def chunk_rows(target, chunk):
        if panels != 2:
            return pl.ds(0, states)
        block = lax.rem(target + chunk, 2)
        return pl.ds(pl.multiple_of(block * width, width), width)

    def cols_of(panel):
        return pl.ds(pl.multiple_of(panel * width, width), width)

    def across(name, ref, slot, step, chunk):
        target = lax.rem(me + step, panels)
        block = panel_block(ref, slot, chunk_rows(target, chunk), own_cols)
        return copy(f"{name}y{step}.{chunk}", block, block, time, target)

    def onward(name, ref, slot, step, chunk):
        source = lax.rem(me - step + panels, panels)
        block = panel_block(ref, slot, chunk_rows(me, chunk), cols_of(source))
        return copy(f"{name}f{step}.{chunk}", block, block, core_peer)

    def beside(name, ref, slot):
        block = ref.at[slot, :, own_cols]
        return copy(f"{name}c", block, block, core_peer)

    def sideways(name, ref, slot):
        block = ref.at[slot, :, own_cols]
        return copy(f"{name}x", block, block, side_peer)

    steps = range(1, panels)
    sym_chunks = (1,) if panels == 2 else (0,)
    all_chunks = (0, 1) if panels == 2 else (0,)

    def products(lhs, rhs, dims, put):
        @pl.loop(0, tiles)
        def _(index):
            cols = pl.ds(pl.multiple_of(index * tile, tile), tile)
            put(cols, dot(lhs[...], rhs(cols), dims))

    def into(ref):
        def put(cols, value):
            ref[:, cols] = value.astype(BF16)
        return put

    def series(cov, info):
        cur[...] = anchor[...]

        @pl.loop(0, TERMS)
        def _(repeat):
            products(info, lambda cols: cur[:, cols], NN, into(inner))

            def put(cols, value):
                cur[:, cols] = (anchor[:, cols].astype(F32) - value).astype(BF16)

            products(cov, lambda cols: inner[:, cols], NN, put)

    def vec_series(start, first, second):
        def step(repeat, vector):
            middle = dot(vector.astype(BF16), first[...])
            return start - dot(middle.astype(BF16), second[...])

        return lax.fori_loop(0, TERMS, step, start)

    def mirror(ref, slot):
        if panels == 2:
            other = pl.ds(pl.multiple_of((1 - me) * width, width), width)
            ref[slot, own_cols, other] = ref[slot, other, own_cols].T

    def start_sym(name, ref, slot):
        for step in steps:
            for chunk in sym_chunks:
                across(name, ref, slot, step, chunk).start()
        beside(name, ref, slot).start()

    def start_moves(name, ref, slot):
        for step in steps:
            for chunk in all_chunks:
                across(name, ref, slot, step, chunk).start()

    def gather_sym(name, ref, slot):
        for step in steps:
            for chunk in sym_chunks:
                across(name, ref, slot, step, chunk).wait_recv()
                onward(name, ref, slot, step, chunk).start()
        beside(name, ref, slot).wait_recv()
        for step in steps:
            for chunk in sym_chunks:
                onward(name, ref, slot, step, chunk).wait_recv()
        mirror(ref, 0)
        mirror(ref, 1)

    def end_sends(name, ref, slot):
        for step in steps:
            for chunk in sym_chunks:
                across(name, ref, slot, step, chunk).wait_send()
                onward(name, ref, slot, step, chunk).wait_send()
        beside(name, ref, slot).wait_send()

    barrier = pltpu.get_barrier_semaphore()
    for at in (core_peer, side_peer, cross_peer):
        pl.semaphore_signal(barrier, inc=1, device_id=(at, me), device_id_type=MESH)
    for step in steps:
        pl.semaphore_signal(
            barrier, inc=1, device_id=(time, lax.rem(me + step, panels)), device_id_type=MESH
        )
    pl.semaphore_wait(barrier, 3 + len(steps))

    @pl.when(core == 0)
    def _():
        s0[0, :, own_cols] = c_ref[...]

    @pl.when(core == 1)
    def _():
        s0[1, :, own_cols] = j_ref[...]

    start_sym("s0", s0, core)
    a0[core, :, own_cols] = a_ref[...]
    start_moves("a0", a0, core)

    @pl.when(core == 1)
    def _():
        beside("a0", a0, 1).start()

    hosts = jnp.broadcast_to(hosts_ref[...].astype(F32) * 2.0, (8, hosts_ref.shape[1])).T[:, :1]
    values = jnp.broadcast_to(values_ref[...], (8, values_ref.shape[1])).T[:, :1]
    spots = lax.broadcasted_iota(jnp.int32, (hosts.shape[0], states), 1).astype(F32)
    paired = jnp.sum(jnp.where(hosts == spots, values, 0.0), axis=0, keepdims=True)
    belief = (eta_ref[...].astype(F32) + paired).astype(BF16).astype(F32)
    v0[core, 0] = jnp.broadcast_to(b_ref[...].astype(F32), (16, states))
    v0[core, 1] = jnp.broadcast_to(belief, (16, states))

    def vec0():
        return copy("v0", v0.at[core], v0.at[core], core_peer)

    vec0().start()
    gather_sym("s0", s0, core)
    vec0().wait_recv()

    def vec1(kind, at, tag):
        block = v1.at[half, kind]
        return copy(f"v1{kind}{tag}", block, block, at)

    vec1_peers = ((core_peer, "c"), (side_peer, "x"), (cross_peer, "d"))

    def late_part(name, cov, info, moves, vecs, addend, store):
        for step in steps:
            across(name, moves, 1, step, 0).wait_recv()
            onward(name, moves, 1, step, 0).start()
        own_rows = me * width

        def rows(cols):
            return moves[1, pl.ds(pl.multiple_of(own_rows + cols.start, tile), tile), :]

        products(cov, rows, NT, into(anchor))
        series(cov, info)
        start = vecs[0, 0] + dot(vecs[1, 1].astype(BF16), cov[...])
        forward = vec_series(start, info, cov)
        for step in steps:
            for chunk in all_chunks[1:]:
                across(name, moves, 1, step, chunk).wait_recv()
                onward(name, moves, 1, step, chunk).start()

        def put(cols, value):
            store(cols, (value + addend(cols).astype(F32)).astype(BF16))

        products(moves.at[1], lambda cols: cur[:, cols], NN, put)
        fresh = dot(forward.astype(BF16), moves[1], NT) + vecs[1, 0]
        return fresh.astype(BF16).astype(F32)

    def early_part(name, cov, info, moves, vecs, addend, store_info, sent_info, store_move):
        anchor[...] = moves[0, :, own_cols]
        series(cov, info)
        products(info, lambda cols: cur[:, cols], NN, into(weighted))
        start = vecs[1, 1] - dot(vecs[0, 0].astype(BF16), info[...])
        backward = vec_series(start, cov, info)
        for step in steps:
            for chunk in all_chunks:
                across(name, moves, 0, step, chunk).wait_recv()

        def put(cols, value):
            store_info(cols, (value + addend(cols).astype(F32)).astype(BF16))

        products(moves.at[0], lambda cols: weighted[:, cols], TN, put)
        sent_info()
        fresh = dot(backward.astype(BF16), moves[0]) + vecs[0, 1]
        if name == "a0":
            beside(name, moves, 1).wait_recv()
        for step in steps:
            for chunk in all_chunks:
                onward(name, moves, 1, step, chunk).wait_recv()
        products(moves.at[1], lambda cols: cur[:, cols], NN, store_move)
        return fresh.astype(BF16).astype(F32)

    info_slot = 2 - half
    cov_slot = 3 * half

    def wide(cols):
        return pl.ds(pl.multiple_of(me * width + cols.start, tile), tile)

    def share_vec(kind, value):
        v1[half, kind] = value
        for at, tag in vec1_peers:
            vec1(kind, at, tag).start()

    @pl.when(core == 0)
    def _():
        def store_info(cols, value):
            s1[info_slot, :, wide(cols)] = value

        def store_move(cols, value):
            a1[half, :, wide(cols)] = value.astype(BF16)

        def sent_info():
            @pl.when(half == 1)
            def _():
                sideways("j1", s1, info_slot).start()
                start_sym("s1", s1, 1)

        fresh = early_part(
            "a0", s0.at[0], s0.at[1], a0, v0, lambda cols: j_ref[:, cols],
            store_info, sent_info, store_move,
        )
        sideways("a1", a1, half).start()
        share_vec(1, fresh)

        @pl.when(half == 0)
        def _():
            start_moves("a1", a1, 0)
            sideways("j1", s1, info_slot).start()
            sideways("j1", s1, 1).wait_recv()
            start_sym("s1", s1, 1)
            sideways("a1", a1, 1).wait_recv()
            beside("a1", a1, 1).start()

        @pl.when(half == 1)
        def _():
            beside("a1", a1, 1).start()
            sideways("a1", a1, 0).wait_recv()
            start_moves("a1", a1, 0)

        gather_sym("s1", s1, 1)
        for kind, at, tag in ((0, core_peer, "c"), (1, side_peer, "x"), (0, cross_peer, "d")):
            vec1(kind, at, tag).wait_recv()

        @pl.when(half == 1)
        def _():
            sideways("j1", s1, 2).wait_recv()

        def put_info(cols, value):
            j_out[:, cols] = value

        def send_info():
            copy("jo", j_out, j_out, core_peer).start()

        fresh = early_part(
            "a1", s1.at[0], s1.at[1], a1, v1, lambda cols: s1[2, :, wide(cols)],
            put_info, send_info, into(a_out),
        )
        copy("ao", a_out, a_out, core_peer).start()
        vec_out[1] = fresh
        copy("eo", vec_out.at[1], vec_out.at[1], core_peer).start()
        copy("co", c_out, c_out, core_peer).wait_recv()
        copy("bo", vec_out.at[0], vec_out.at[0], core_peer).wait_recv()
        for step in steps:
            for chunk in all_chunks:
                across("a0", a0, 0, step, chunk).wait_send()
                across("a1", a1, 0, step, chunk).wait_send()
        end_sends("s1", s1, 1)
        sideways("j1", s1, info_slot).wait_send()
        sideways("a1", a1, half).wait_send()
        beside("a1", a1, 1).wait_send()
        for at, tag in vec1_peers:
            vec1(1, at, tag).wait_send()
        copy("jo", j_out, j_out, core_peer).wait_send()
        copy("ao", a_out, a_out, core_peer).wait_send()
        copy("eo", vec_out.at[1], vec_out.at[1], core_peer).wait_send()

    @pl.when(core == 1)
    def _():
        def store_cov(cols, value):
            s1[cov_slot, :, wide(cols)] = value

        fresh = late_part(
            "a0", s0.at[0], s0.at[1], a0, v0, lambda cols: c_ref[:, cols], store_cov
        )

        @pl.when(half == 0)
        def _():
            sideways("c1", s1, 0).start()
            start_sym("s1", s1, 0)

        share_vec(0, fresh)

        @pl.when(half == 1)
        def _():
            sideways("c1", s1, 0).wait_recv()
            start_sym("s1", s1, 0)

        beside("a1", a1, 1).wait_recv()
        start_moves("a1", a1, 1)

        @pl.when(half == 1)
        def _():
            sideways("c1", s1, 3).start()

        gather_sym("s1", s1, 0)
        for kind, at, tag in ((1, core_peer, "c"), (0, side_peer, "x"), (1, cross_peer, "d")):
            vec1(kind, at, tag).wait_recv()

        @pl.when(half == 0)
        def _():
            sideways("c1", s1, 3).wait_recv()

        def put_cov(cols, value):
            c_out[:, cols] = value

        fresh = late_part(
            "a1", s1.at[0], s1.at[1], a1, v1, lambda cols: s1[3, :, wide(cols)], put_cov
        )
        copy("co", c_out, c_out, core_peer).start()
        vec_out[0] = fresh
        copy("bo", vec_out.at[0], vec_out.at[0], core_peer).start()
        copy("jo", j_out, j_out, core_peer).wait_recv()
        copy("ao", a_out, a_out, core_peer).wait_recv()
        copy("eo", vec_out.at[1], vec_out.at[1], core_peer).wait_recv()
        for step in steps:
            for chunk in all_chunks:
                for name, ref in (("a0", a0), ("a1", a1)):
                    across(name, ref, 1, step, chunk).wait_send()
                    onward(name, ref, 1, step, chunk).wait_send()
        beside("a0", a0, 1).wait_send()
        end_sends("s1", s1, 0)
        sideways("c1", s1, cov_slot).wait_send()
        for at, tag in vec1_peers:
            vec1(0, at, tag).wait_send()
        copy("co", c_out, c_out, core_peer).wait_send()
        copy("bo", vec_out.at[0], vec_out.at[0], core_peer).wait_send()

    end_sends("s0", s0, core)
    vec0().wait_send()


def local(panels, transition, drift, spread, belief, precision, probe_hosts, probe_values):
    states, width = transition.shape[1:]
    panel = jax.ShapeDtypeStruct((states, width), BF16)
    vmem = pl.BlockSpec(memory_space=pltpu.VMEM)
    square = (states, states)
    count = 24 + 16 * (panels - 1)
    combine = 2 * states * states * width
    a, c, j, vecs = pl.pallas_call(
        functools.partial(kernel, panels, {}),
        out_shape=(panel, panel, panel, jax.ShapeDtypeStruct((2, 16, states), F32)),
        in_specs=[vmem] * 7,
        out_specs=(vmem,) * 4,
        scratch_shapes=[
            pltpu.VMEM((2,) + square, BF16),
            pltpu.VMEM((2,) + square, BF16),
            pltpu.VMEM((4,) + square, BF16),
            pltpu.VMEM((2,) + square, BF16),
            pltpu.VMEM((2, 2, 16, states), F32),
            pltpu.VMEM((2, 2, 16, states), F32),
            pltpu.VMEM((states, width), BF16),
            pltpu.VMEM((states, width), BF16),
            pltpu.VMEM((states, width), BF16),
            pltpu.VMEM((states, width), BF16),
            pltpu.SemaphoreType.DMA((count,)),
            pltpu.SemaphoreType.DMA((count,)),
        ],
        compiler_params=pltpu.CompilerParams(
            collective_id=0, has_side_effects=True, vmem_limit_bytes=56 * 2**20
        ),
        cost_estimate=pl.CostEstimate(
            flops=18 * combine, bytes_accessed=12 * states * width, transcendentals=0
        ),
    )(
        transition[0], spread[0], precision[0], drift, belief, probe_hosts, probe_values
    )
    fresh = vecs[:, 0].astype(BF16)
    return a[None], fresh[0:1], c[None], fresh[1:2], j[None]


def solution(mesh):
    matrix = P("tm", None, "panel")
    vector = P("tm", None)
    return jax.shard_map(
        functools.partial(local, mesh.shape["panel"]),
        mesh=mesh,
        in_specs=(matrix, vector, matrix, vector, matrix, vector, vector),
        out_specs=(matrix, vector, matrix, vector, matrix),
        check_vma=False,
    )
```

profile of v0, /device:TPU:31, one launch (start us, length us, event | category | flops | bytes accessed | tf_op | source)
XLA Modules:
  0.0 113.7 jit_solution(5304290971848261849)
XLA Ops:
  0.6 106.6 %shard_map.110 = (bf16[1024,512]{1,0:T(8,128)(2,1)}, bf16[1024,512]{1,0:T(8,128)(2,1)}, bf16[1024,512]{1,0:T(8,128)(2,1)}, f32[2,16,1024]{2,1,0:T(8,128)}) custom-call(bf16[1024,512]{1,0:T(8,128)(2,1)} %bitcast.13, bf16[1024,512]{1,0:T(8,128)(2,1)} %bitcast.14, bf16[1024,512]{1,0:T(8,128)(2,1)} %bitcast.15, bf16[1,1024]{1,0:T(2,128)(2,1)} %b_ref.1, ...), custom_call_target="tpu_custom_call" | custom-call | flops 19327352832 | bytes 6291456 | tf_op jit(solution)/shard_map/pallas_call | solution.py:403
  107.2 0.9 convert.3
  108.1 0.6 slice_bitcast_fusion
  108.7 0.0 copy-start.1
  108.7 2.4 %copy.15 = bf16[1,1024,512]{2,1,0:T(8,128)(2,1)} copy(bf16[1,1024,512]{2,1,0:T(8,128)(2,1)} %bitcast.12) | data formatting | bytes 2097152
  111.1 0.0 copy-done.1
  111.1 0.0 copy-start
  111.1 1.0 copy.16
  112.1 0.6 copy-done
  112.7 1.0 copy.17
Async XLA Ops:
  108.7 2.4 %copy-start.1 = (bf16[1024,512]{1,0:T(8,128)(2,1)S(1)}, bf16[1024,512]{1,0:T(8,128)(2,1)}, u32[]{:S(2)}) copy-start(bf16[1024,512]{1,0:T(8,128)(2,1)} %get-tuple-element.11) | copy-start | bytes 3145732
  111.1 1.6 %copy-start = (bf16[1024,512]{1,0:T(8,128)(2,1)S(1)}, bf16[1024,512]{1,0:T(8,128)(2,1)}, u32[]{:S(2)}) copy-start(bf16[1024,512]{1,0:T(8,128)(2,1)} %get-tuple-element.12) | copy-start | bytes 3145732
where the time goes:
time: 114 us
  Pallas kernels  107 us (94%)
  local copies, waits for them, and re-layouts  5.53 us (5%)
    pallas_call x1, Pallas kernels, local(): pl.pallas_call(functools.partial(kernel, panels, {}), out_shape=(panel, p...  107 us
    unnamed x7, local copies, waits for them, and re-layouts  4.93 us

commit v1 on v0

--- a/solution.py
+++ b/solution.py
@@ -72,17 +72,18 @@
         block = panel_block(ref, slot, chunk_rows(me, chunk), cols_of(source))
         return copy(f"{name}f{step}.{chunk}", block, block, core_peer)
 
-    def beside(name, ref, slot):
-        block = ref.at[slot, :, own_cols]
-        return copy(f"{name}c", block, block, core_peer)
-
-    def sideways(name, ref, slot):
-        block = ref.at[slot, :, own_cols]
-        return copy(f"{name}x", block, block, side_peer)
+    def beside(name, ref, slot, chunk):
+        block = panel_block(ref, slot, chunk_rows(me + 1, chunk), own_cols)
+        return copy(f"{name}c{chunk}", block, block, core_peer)
+
+    def sideways(name, ref, slot, chunk, at=side_peer):
+        block = panel_block(ref, slot, chunk_rows(me + 1, chunk), own_cols)
+        return copy(f"{name}x{chunk}", block, block, at)
 
     steps = range(1, panels)
     sym_chunks = (1,) if panels == 2 else (0,)
     all_chunks = (0, 1) if panels == 2 else (0,)
+    sym_first = all_chunks[::-1]
 
     def products(lhs, rhs, dims, put):
         @pl.loop(0, tiles)
@@ -119,23 +120,24 @@
             other = pl.ds(pl.multiple_of((1 - me) * width, width), width)
             ref[slot, own_cols, other] = ref[slot, other, own_cols].T
 
-    def start_sym(name, ref, slot):
-        for step in steps:
-            for chunk in sym_chunks:
+    def start_across(name, ref, slot, chunks):
+        for step in steps:
+            for chunk in chunks:
                 across(name, ref, slot, step, chunk).start()
-        beside(name, ref, slot).start()
-
-    def start_moves(name, ref, slot):
-        for step in steps:
-            for chunk in all_chunks:
-                across(name, ref, slot, step, chunk).start()
-
-    def gather_sym(name, ref, slot):
+
+    def start_beside(name, ref, slot, chunks=sym_first):
+        for chunk in chunks:
+            beside(name, ref, slot, chunk).start()
+
+    def pass_sym(name, ref, slot):
         for step in steps:
             for chunk in sym_chunks:
                 across(name, ref, slot, step, chunk).wait_recv()
                 onward(name, ref, slot, step, chunk).start()
-        beside(name, ref, slot).wait_recv()
+
+    def gather_sym(name, ref, slot):
+        for chunk in sym_first:
+            beside(name, ref, slot, chunk).wait_recv()
         for step in steps:
             for chunk in sym_chunks:
                 onward(name, ref, slot, step, chunk).wait_recv()
@@ -145,9 +147,11 @@
     def end_sends(name, ref, slot):
         for step in steps:
             for chunk in sym_chunks:
-                across(name, ref, slot, step, chunk).wait_send()
+                if name != "s0":
+                    across(name, ref, slot, step, chunk).wait_send()
                 onward(name, ref, slot, step, chunk).wait_send()
-        beside(name, ref, slot).wait_send()
+        for chunk in sym_first:
+            beside(name, ref, slot, chunk).wait_send()
 
     barrier = pltpu.get_barrier_semaphore()
     for at in (core_peer, side_peer, cross_peer):
@@ -166,13 +170,13 @@
     def _():
         s0[1, :, own_cols] = j_ref[...]
 
-    start_sym("s0", s0, core)
+    start_across("s0", s0, core, sym_chunks)
+    start_beside("s0", s0, core)
     a0[core, :, own_cols] = a_ref[...]
-    start_moves("a0", a0, core)
 
     @pl.when(core == 1)
     def _():
-        beside("a0", a0, 1).start()
+        start_beside("a0", a0, 1, all_chunks)
 
     hosts = jnp.broadcast_to(hosts_ref[...].astype(F32) * 2.0, (8, hosts_ref.shape[1])).T[:, :1]
     values = jnp.broadcast_to(values_ref[...], (8, values_ref.shape[1])).T[:, :1]
@@ -186,6 +190,11 @@
         return copy("v0", v0.at[core], v0.at[core], core_peer)
 
     vec0().start()
+    for step in steps:
+        for chunk in sym_chunks:
+            across("s0", s0, core, step, chunk).wait_send()
+    start_across("a0", a0, core, all_chunks)
+    pass_sym("s0", s0, core)
     gather_sym("s0", s0, core)
     vec0().wait_recv()
 
@@ -195,7 +204,17 @@
 
     vec1_peers = ((core_peer, "c"), (side_peer, "x"), (cross_peer, "d"))
 
-    def late_part(name, cov, info, moves, vecs, addend, store):
+    def late_part(name, cov, info, moves, vecs, addend, ready, store):
+        start = vecs[0, 0] + dot(vecs[1, 1].astype(BF16), cov[...])
+        forward = vec_series(start, info, cov)
+        if name == "a1":
+            @pl.when(half == 0)
+            def _():
+                for chunk in all_chunks:
+                    sideways("a1", a1, 1, chunk).wait_recv()
+                    start_across("a1", a1, 1, (chunk,))
+                    beside("b1", a1, 1, chunk).start()
+
         for step in steps:
             across(name, moves, 1, step, 0).wait_recv()
             onward(name, moves, 1, step, 0).start()
@@ -206,13 +225,13 @@
 
         products(cov, rows, NT, into(anchor))
         series(cov, info)
-        start = vecs[0, 0] + dot(vecs[1, 1].astype(BF16), cov[...])
-        forward = vec_series(start, info, cov)
         for step in steps:
             for chunk in all_chunks[1:]:
                 across(name, moves, 1, step, chunk).wait_recv()
                 onward(name, moves, 1, step, chunk).start()
 
+        ready()
+
         def put(cols, value):
             store(cols, (value + addend(cols).astype(F32)).astype(BF16))
 
@@ -220,7 +239,7 @@
         fresh = dot(forward.astype(BF16), moves[1], NT) + vecs[1, 0]
         return fresh.astype(BF16).astype(F32)
 
-    def early_part(name, cov, info, moves, vecs, addend, store_info, sent_info, store_move):
+    def early_part(name, cov, info, moves, vecs, addend, ready_info, store_info, sent_info, store_move):
         anchor[...] = moves[0, :, own_cols]
         series(cov, info)
         products(info, lambda cols: cur[:, cols], NN, into(weighted))
@@ -230,6 +249,8 @@
             for chunk in all_chunks:
                 across(name, moves, 0, step, chunk).wait_recv()
 
+        ready_info()
+
         def put(cols, value):
             store_info(cols, (value + addend(cols).astype(F32)).astype(BF16))
 
@@ -237,7 +258,14 @@
         sent_info()
         fresh = dot(backward.astype(BF16), moves[0]) + vecs[0, 1]
         if name == "a0":
-            beside(name, moves, 1).wait_recv()
+            for chunk in all_chunks:
+                beside(name, moves, 1, chunk).wait_recv()
+        else:
+            @pl.when(half == 0)
+            def _():
+                for chunk in all_chunks:
+                    beside("b1", moves, 1, chunk).wait_recv()
+
         for step in steps:
             for chunk in all_chunks:
                 onward(name, moves, 1, step, chunk).wait_recv()
@@ -266,38 +294,65 @@
         def sent_info():
             @pl.when(half == 1)
             def _():
-                sideways("j1", s1, info_slot).start()
-                start_sym("s1", s1, 1)
+                sideways("j1", s1, 1, sym_first[0]).start()
+                start_across("s1", s1, 1, sym_chunks)
+                start_beside("s1", s1, 1)
 
         fresh = early_part(
             "a0", s0.at[0], s0.at[1], a0, v0, lambda cols: j_ref[:, cols],
-            store_info, sent_info, store_move,
+            lambda: None, store_info, sent_info, store_move,
         )
-        sideways("a1", a1, half).start()
         share_vec(1, fresh)
 
         @pl.when(half == 0)
         def _():
-            start_moves("a1", a1, 0)
-            sideways("j1", s1, info_slot).start()
-            sideways("j1", s1, 1).wait_recv()
-            start_sym("s1", s1, 1)
-            sideways("a1", a1, 1).wait_recv()
-            beside("a1", a1, 1).start()
+            for chunk in all_chunks:
+                sideways("a1", a1, 0, chunk).start()
+            start_across("a1", a1, 0, all_chunks[:1])
+            sideways("j1", s1, 1, sym_first[0]).wait_recv()
+            start_across("s1", s1, 1, sym_chunks)
+            start_beside("s1", s1, 1, sym_first[:1])
 
         @pl.when(half == 1)
         def _():
-            beside("a1", a1, 1).start()
-            sideways("a1", a1, 0).wait_recv()
-            start_moves("a1", a1, 0)
+            start_beside("a1", a1, 1, all_chunks)
+            sideways("j1", s1, 1, sym_first[0]).wait_send()
+            for chunk in sym_first[1:]:
+                sideways("j1", s1, 1, chunk).start()
+            sideways("a1", a1, 1, 0, cross_peer).start()
+
+        pass_sym("s1", s1, 1)
+
+        @pl.when(half == 0)
+        def _():
+            for chunk in sym_first[1:]:
+                sideways("j1", s1, 1, chunk).wait_recv()
+                start_beside("s1", s1, 1, (chunk,))
+            start_across("a1", a1, 0, all_chunks[1:])
+
+        @pl.when(half == 1)
+        def _():
+            for chunk in all_chunks[1:]:
+                sideways("j1", s1, 1, sym_first[1]).wait_send()
+                sideways("a1", a1, 1, chunk, cross_peer).start()
+            for chunk in all_chunks:
+                sideways("a1", a1, 0, chunk).wait_recv()
+                start_across("a1", a1, 0, (chunk,))
 
         gather_sym("s1", s1, 1)
         for kind, at, tag in ((0, core_peer, "c"), (1, side_peer, "x"), (0, cross_peer, "d")):
             vec1(kind, at, tag).wait_recv()
 
-        @pl.when(half == 1)
-        def _():
-            sideways("j1", s1, 2).wait_recv()
+        @pl.when(half == 0)
+        def _():
+            for chunk in all_chunks:
+                sideways("j1", s1, 2, chunk).start()
+
+        def late_info():
+            @pl.when(half == 1)
+            def _():
+                for chunk in all_chunks:
+                    sideways("j1", s1, 2, chunk).wait_recv()
 
         def put_info(cols, value):
             j_out[:, cols] = value
@@ -307,7 +362,7 @@
 
         fresh = early_part(
             "a1", s1.at[0], s1.at[1], a1, v1, lambda cols: s1[2, :, wide(cols)],
-            put_info, send_info, into(a_out),
+            late_info, put_info, send_info, into(a_out),
         )
         copy("ao", a_out, a_out, core_peer).start()
         vec_out[1] = fresh
@@ -319,9 +374,19 @@
                 across("a0", a0, 0, step, chunk).wait_send()
                 across("a1", a1, 0, step, chunk).wait_send()
         end_sends("s1", s1, 1)
-        sideways("j1", s1, info_slot).wait_send()
-        sideways("a1", a1, half).wait_send()
-        beside("a1", a1, 1).wait_send()
+
+        @pl.when(half == 0)
+        def _():
+            for chunk in all_chunks:
+                sideways("j1", s1, 2, chunk).wait_send()
+                sideways("a1", a1, 0, chunk).wait_send()
+
+        @pl.when(half == 1)
+        def _():
+            for chunk in all_chunks:
+                sideways("a1", a1, 1, chunk, cross_peer).wait_send()
+                beside("a1", a1, 1, chunk).wait_send()
+
         for at, tag in vec1_peers:
             vec1(1, at, tag).wait_send()
         copy("jo", j_out, j_out, core_peer).wait_send()
@@ -334,41 +399,55 @@
             s1[cov_slot, :, wide(cols)] = value
 
         fresh = late_part(
-            "a0", s0.at[0], s0.at[1], a0, v0, lambda cols: c_ref[:, cols], store_cov
+            "a0", s0.at[0], s0.at[1], a0, v0, lambda cols: c_ref[:, cols],
+            lambda: None, store_cov
         )
 
         @pl.when(half == 0)
         def _():
-            sideways("c1", s1, 0).start()
-            start_sym("s1", s1, 0)
+            start_across("s1", s1, 0, sym_chunks)
+            for chunk in sym_first:
+                sideways("c1", s1, 0, chunk).start()
+            start_beside("s1", s1, 0)
 
         share_vec(0, fresh)
 
         @pl.when(half == 1)
         def _():
-            sideways("c1", s1, 0).wait_recv()
-            start_sym("s1", s1, 0)
-
-        beside("a1", a1, 1).wait_recv()
-        start_moves("a1", a1, 1)
+            for chunk in all_chunks:
+                beside("a1", a1, 1, chunk).wait_recv()
+            start_across("a1", a1, 1, all_chunks[:1])
+            sideways("c1", s1, 0, sym_first[0]).wait_recv()
+            start_across("s1", s1, 0, sym_chunks)
+            start_beside("s1", s1, 0, sym_first[:1])
+
+        pass_sym("s1", s1, 0)
 
         @pl.when(half == 1)
         def _():
-            sideways("c1", s1, 3).start()
+            for chunk in sym_first[1:]:
+                sideways("c1", s1, 0, chunk).wait_recv()
+                start_beside("s1", s1, 0, (chunk,))
+            start_across("a1", a1, 1, all_chunks[1:])
+            for chunk in all_chunks:
+                sideways("c1", s1, 3, chunk).start()
 
         gather_sym("s1", s1, 0)
         for kind, at, tag in ((1, core_peer, "c"), (0, side_peer, "x"), (1, cross_peer, "d")):
             vec1(kind, at, tag).wait_recv()
 
-        @pl.when(half == 0)
-        def _():
-            sideways("c1", s1, 3).wait_recv()
+        def late_cov():
+            @pl.when(half == 0)
+            def _():
+                for chunk in all_chunks:
+                    sideways("c1", s1, 3, chunk).wait_recv()
 
         def put_cov(cols, value):
             c_out[:, cols] = value
 
         fresh = late_part(
-            "a1", s1.at[0], s1.at[1], a1, v1, lambda cols: s1[3, :, wide(cols)], put_cov
+            "a1", s1.at[0], s1.at[1], a1, v1, lambda cols: s1[3, :, wide(cols)],
+            late_cov, put_cov
         )
         copy("co", c_out, c_out, core_peer).start()
         vec_out[0] = fresh
@@ -381,9 +460,16 @@
                 for name, ref in (("a0", a0), ("a1", a1)):
                     across(name, ref, 1, step, chunk).wait_send()
                     onward(name, ref, 1, step, chunk).wait_send()
-        beside("a0", a0, 1).wait_send()
+        for chunk in all_chunks:
+            beside("a0", a0, 1, chunk).wait_send()
+            sideways("c1", s1, cov_slot, chunk).wait_send()
+
+        @pl.when(half == 0)
+        def _():
+            for chunk in all_chunks:
+                beside("b1", a1, 1, chunk).wait_send()
+
         end_sends("s1", s1, 0)
-        sideways("c1", s1, cov_slot).wait_send()
         for at, tag in vec1_peers:
             vec1(0, at, tag).wait_send()
         copy("co", c_out, c_out, core_peer).wait_send()
@@ -391,6 +477,19 @@
 
     end_sends("s0", s0, core)
     vec0().wait_send()
+
+
+def place(a_ref, c_ref, j_ref, vec_ref, a_out, b_out, c_out, eta_out, j_out, sems):
+    moves = [
+        pltpu.make_async_copy(src, dst, sems.at[index])
+        for index, (src, dst) in enumerate(((a_ref, a_out), (c_ref, c_out), (j_ref, j_out)))
+    ]
+    for move in moves:
+        move.start()
+    b_out[...] = vec_ref[0, 0:1].astype(BF16)
+    eta_out[...] = vec_ref[1, 0:1].astype(BF16)
+    for move in moves:
+        move.wait()
 
 
 def local(panels, transition, drift, spread, belief, precision, probe_hosts, probe_values):
@@ -398,7 +497,7 @@
     panel = jax.ShapeDtypeStruct((states, width), BF16)
     vmem = pl.BlockSpec(memory_space=pltpu.VMEM)
     square = (states, states)
-    count = 24 + 16 * (panels - 1)
+    count = 48 + 16 * (panels - 1)
     combine = 2 * states * states * width
     a, c, j, vecs = pl.pallas_call(
         functools.partial(kernel, panels, {}),
@@ -428,8 +527,19 @@
     )(
         transition[0], spread[0], precision[0], drift, belief, probe_hosts, probe_values
     )
-    fresh = vecs[:, 0].astype(BF16)
-    return a[None], fresh[0:1], c[None], fresh[1:2], j[None]
+    anywhere = pl.BlockSpec(memory_space=pl.ANY)
+    row = jax.ShapeDtypeStruct((1, states), BF16)
+    a, b, c, eta, j = pl.pallas_call(
+        place,
+        out_shape=(panel, row, panel, row, panel),
+        in_specs=[anywhere] * 3 + [vmem],
+        out_specs=(anywhere, vmem, anywhere, vmem, anywhere),
+        scratch_shapes=[pltpu.SemaphoreType.DMA((3,))],
+        cost_estimate=pl.CostEstimate(
+            flops=0, bytes_accessed=12 * states * width, transcendentals=0
+        ),
+    )(a, c, j, vecs)
+    return a[None], b, c[None], eta, j[None]
 
 
 def solution(mesh):

time: 114 us -> 192 us (1.68)
  the two profiles are of different devices: /device:TPU:31 before, /device:TPU:0 now
where the time goes in v1:
time: 192 us
  Pallas kernels  191 us (99%)
    pallas_call x1, Pallas kernels, local(): pl.pallas_call(place, out_shape=(panel, row, panel, row, panel), in_specs...  97.9 us
    pallas_call x1, Pallas kernels, local(): pl.pallas_call(functools.partial(kernel, panels, {}), out_shape=(panel, p...  92.8 us

profile of v1, /device:TPU:0, one launch (start us, length us, event | category | flops | bytes accessed | tf_op | source)
XLA Modules:
  0.0 191.6 jit_solution(5255428266767878627)
XLA Ops:
  0.6 92.8 %shard_map.110 = (bf16[1024,512]{1,0:T(8,128)(2,1)}, bf16[1024,512]{1,0:T(8,128)(2,1)}, bf16[1024,512]{1,0:T(8,128)(2,1)}, f32[2,16,1024]{2,1,0:T(8,128)}) custom-call(bf16[1024,512]{1,0:T(8,128)(2,1)} %bitcast.6, bf16[1024,512]{1,0:T(8,128)(2,1)} %bitcast.7, bf16[1024,512]{1,0:T(8,128)(2,1)} %bitcast.8, bf16[1,1024]{1,0:T(2,128)(2,1)} %b_ref.1, ...), custom_call_target="tpu_custom_call" | custom-call | flops 19327352832 | bytes 6291456 | tf_op jit(solution)/shard_map/pallas_call | solution.py:502
  93.5 97.9 %shard_map.111 = (bf16[1024,512]{1,0:T(8,128)(2,1)}, bf16[1,1024]{1,0:T(2,128)(2,1)}, bf16[1024,512]{1,0:T(8,128)(2,1)}, bf16[1,1024]{1,0:T(2,128)(2,1)}, bf16[1024,512]{1,0:T(8,128)(2,1)}) custom-call(bf16[1024,512]{1,0:T(8,128)(2,1)} %get-tuple-element.14.a_ref, bf16[1024,512]{1,0:T(8,128)(2,1)} %get-tuple-element.15.c_ref, ...), custom_call_target="tpu_custom_call" | custom-call | bytes 6291456 | tf_op jit(solution)/shard_map/pallas_call | solution.py:532

commit v2 on v1

--- a/solution.py
+++ b/solution.py
@@ -86,9 +86,8 @@
     sym_first = all_chunks[::-1]
 
     def products(lhs, rhs, dims, put):
-        @pl.loop(0, tiles)
-        def _(index):
-            cols = pl.ds(pl.multiple_of(index * tile, tile), tile)
+        for index in range(tiles):
+            cols = pl.ds(index * tile, tile)
             put(cols, dot(lhs[...], rhs(cols), dims))
 
     def into(ref):
@@ -479,17 +478,25 @@
     vec0().wait_send()
 
 
-def place(a_ref, c_ref, j_ref, vec_ref, a_out, b_out, c_out, eta_out, j_out, sems):
-    moves = [
-        pltpu.make_async_copy(src, dst, sems.at[index])
-        for index, (src, dst) in enumerate(((a_ref, a_out), (c_ref, c_out), (j_ref, j_out)))
-    ]
-    for move in moves:
-        move.start()
+def place(a_ref, c_ref, j_ref, vec_ref, a_out, b_out, c_out, eta_out, j_out, held, sems):
+    pieces = held.shape[1]
+    rows = held.shape[2]
+    fetches, sends = [], []
+    for index, (src, dst) in enumerate(((a_ref, a_out), (c_ref, c_out), (j_ref, j_out))):
+        for piece in range(pieces):
+            block = pl.ds(piece * rows, rows)
+            slot = held.at[index, piece]
+            fetches.append(pltpu.make_async_copy(src.at[block], slot, sems.at[0, index, piece]))
+            sends.append(pltpu.make_async_copy(slot, dst.at[block], sems.at[1, index, piece]))
+    for fetch in fetches:
+        fetch.start()
     b_out[...] = vec_ref[0, 0:1].astype(BF16)
     eta_out[...] = vec_ref[1, 0:1].astype(BF16)
-    for move in moves:
-        move.wait()
+    for fetch, send in zip(fetches, sends):
+        fetch.wait()
+        send.start()
+    for send in sends:
+        send.wait()
 
 
 def local(panels, transition, drift, spread, belief, precision, probe_hosts, probe_values):
@@ -534,7 +541,10 @@
         out_shape=(panel, row, panel, row, panel),
         in_specs=[anywhere] * 3 + [vmem],
         out_specs=(anywhere, vmem, anywhere, vmem, anywhere),
-        scratch_shapes=[pltpu.SemaphoreType.DMA((3,))],
+        scratch_shapes=[
+            pltpu.VMEM((3, 2, states // 2, width), BF16),
+            pltpu.SemaphoreType.DMA((2, 3, 2)),
+        ],
         cost_estimate=pl.CostEstimate(
             flops=0, bytes_accessed=12 * states * width, transcendentals=0
         ),

time: 192 us -> 95.8 us (0.50)
  Pallas kernels: 191 us -> 94.8 us
    pallas_call x1, Pallas kernels: 97.9 us -> 4.3 us  [local(): pl.pallas_call(place, out_shape=(panel, row, panel, row, panel), in_specs...]
    pallas_call x1, Pallas kernels: 92.8 us -> 90.5 us  [local(): pl.pallas_call(functools.partial(kernel, panels, {}), out_shape=(panel, p...]
where the time goes in v2:
time: 95.8 us; the launch traced here: 95.6 us
  Pallas kernels  94.8 us (99%)
    pallas_call x1, Pallas kernels, local(): pl.pallas_call(functools.partial(kernel, panels, {}), out_shape=(panel, p...  90.5 us
    pallas_call x1, Pallas kernels, local(): pl.pallas_call(place, out_shape=(panel, row, panel, row, panel), in_specs...  4.3 us

profile of v2, /device:TPU:0, one launch (start us, length us, event | category | flops | bytes accessed | tf_op | source)
XLA Modules:
  0.0 95.6 jit_solution(12986024229807692700)
XLA Ops:
  0.6 90.5 %shard_map.110 = (bf16[1024,512]{1,0:T(8,128)(2,1)}, bf16[1024,512]{1,0:T(8,128)(2,1)}, bf16[1024,512]{1,0:T(8,128)(2,1)}, f32[2,16,1024]{2,1,0:T(8,128)}) custom-call(bf16[1024,512]{1,0:T(8,128)(2,1)} %bitcast.6, bf16[1024,512]{1,0:T(8,128)(2,1)} %bitcast.7, bf16[1024,512]{1,0:T(8,128)(2,1)} %bitcast.8, bf16[1,1024]{1,0:T(2,128)(2,1)} %b_ref.1, ...), custom_call_target="tpu_custom_call" | custom-call | flops 19327352832 | bytes 6291456 | tf_op jit(solution)/shard_map/pallas_call | solution.py:509
  91.2 4.3 %shard_map.111 = (bf16[1024,512]{1,0:T(8,128)(2,1)}, bf16[1,1024]{1,0:T(2,128)(2,1)}, bf16[1024,512]{1,0:T(8,128)(2,1)}, bf16[1,1024]{1,0:T(2,128)(2,1)}, bf16[1024,512]{1,0:T(8,128)(2,1)}) custom-call(bf16[1024,512]{1,0:T(8,128)(2,1)} %get-tuple-element.14.a_ref, bf16[1024,512]{1,0:T(8,128)(2,1)} %get-tuple-element.15.c_ref, ...), custom_call_target="tpu_custom_call" | custom-call | bytes 6291456 | tf_op jit(solution)/shard_map/pallas_call | solution.py:539

commit v3 on v2

--- a/solution.py
+++ b/solution.py
@@ -25,7 +25,7 @@
     panels, names,
     a_ref, c_ref, j_ref, b_ref, eta_ref, hosts_ref, values_ref,
     a_out, c_out, j_out, vec_out,
-    s0, a0, s1, a1, v0, v1, anchor, cur, inner, weighted, send_sem, recv_sem,
+    s0, a0, s1, a1, v0, v1, anchor, cur, inner, weighted, send_sem, recv_sem, place_sem,
 ):
     states, width = a_ref.shape
     tile = min(width, 256)
@@ -152,6 +152,29 @@
         for chunk in sym_first:
             beside(name, ref, slot, chunk).wait_send()
 
+    def keep(name, src, dst, index):
+        cols = pl.ds(index * tile, tile)
+        return pltpu.make_async_copy(
+            src.at[:, cols], dst.at[:, cols], place_sem.at[sem(f"{name}{index}")]
+        )
+
+    def share(name, src, dst, index):
+        cols = pl.ds(index * tile, tile)
+        return copy(f"{name}{index}", src.at[:, cols], dst.at[:, cols], core_peer)
+
+    def start_result(name, src, dst, cols):
+        share(name, src, dst, cols.start // tile).start()
+        keep(name, src, dst, cols.start // tile).start()
+
+    def end_results(name, src, dst):
+        for index in range(tiles):
+            keep(name, src, dst, index).wait()
+            share(name, src, dst, index).wait_send()
+
+    def end_arrivals(name, src, dst):
+        for index in range(tiles):
+            share(name, src, dst, index).wait_recv()
+
     barrier = pltpu.get_barrier_semaphore()
     for at in (core_peer, side_peer, cross_peer):
         pl.semaphore_signal(barrier, inc=1, device_id=(at, me), device_id_type=MESH)
@@ -192,7 +215,7 @@
     for step in steps:
         for chunk in sym_chunks:
             across("s0", s0, core, step, chunk).wait_send()
-    start_across("a0", a0, core, all_chunks)
+    start_across("a0", a0, core, all_chunks[:1])
     pass_sym("s0", s0, core)
     gather_sym("s0", s0, core)
     vec0().wait_recv()
@@ -202,6 +225,12 @@
         return copy(f"v1{kind}{tag}", block, block, at)
 
     vec1_peers = ((core_peer, "c"), (side_peer, "x"), (cross_peer, "d"))
+
+    def take_move(chunks):
+        for chunk in chunks:
+            sideways("a1", a1, 1, chunk).wait_recv()
+            start_across("a1", a1, 1, (chunk,))
+            beside("b1", a1, 1, chunk).start()
 
     def late_part(name, cov, info, moves, vecs, addend, ready, store):
         start = vecs[0, 0] + dot(vecs[1, 1].astype(BF16), cov[...])
@@ -209,13 +238,13 @@
         if name == "a1":
             @pl.when(half == 0)
             def _():
-                for chunk in all_chunks:
-                    sideways("a1", a1, 1, chunk).wait_recv()
-                    start_across("a1", a1, 1, (chunk,))
-                    beside("b1", a1, 1, chunk).start()
+                take_move(all_chunks[1:])
 
         for step in steps:
             across(name, moves, 1, step, 0).wait_recv()
+        if name == "a0":
+            start_across("a0", a0, 1, all_chunks[1:])
+        for step in steps:
             onward(name, moves, 1, step, 0).start()
         own_rows = me * width
 
@@ -239,11 +268,26 @@
         return fresh.astype(BF16).astype(F32)
 
     def early_part(name, cov, info, moves, vecs, addend, ready_info, store_info, sent_info, store_move):
+        def vector():
+            start = vecs[1, 1] - dot(vecs[0, 0].astype(BF16), info[...])
+            return vec_series(start, cov, info)
+
+        if name == "a1":
+            backward = vector()
+
+            @pl.when(half == 1)
+            def _():
+                for chunk in all_chunks:
+                    sideways("a1", a1, 0, chunk).wait_recv()
+                    start_across("a1", a1, 0, (chunk,))
+
         anchor[...] = moves[0, :, own_cols]
         series(cov, info)
+        if name == "a0":
+            start_across("a0", a0, 0, all_chunks[1:])
         products(info, lambda cols: cur[:, cols], NN, into(weighted))
-        start = vecs[1, 1] - dot(vecs[0, 0].astype(BF16), info[...])
-        backward = vec_series(start, cov, info)
+        if name == "a0":
+            backward = vector()
         for step in steps:
             for chunk in all_chunks:
                 across(name, moves, 0, step, chunk).wait_recv()
@@ -305,38 +349,36 @@
 
         @pl.when(half == 0)
         def _():
-            for chunk in all_chunks:
-                sideways("a1", a1, 0, chunk).start()
-            start_across("a1", a1, 0, all_chunks[:1])
             sideways("j1", s1, 1, sym_first[0]).wait_recv()
             start_across("s1", s1, 1, sym_chunks)
             start_beside("s1", s1, 1, sym_first[:1])
+            sideways("a1", a1, 0, 0).start()
 
         @pl.when(half == 1)
         def _():
             start_beside("a1", a1, 1, all_chunks)
             sideways("j1", s1, 1, sym_first[0]).wait_send()
-            for chunk in sym_first[1:]:
-                sideways("j1", s1, 1, chunk).start()
             sideways("a1", a1, 1, 0, cross_peer).start()
 
         pass_sym("s1", s1, 1)
 
         @pl.when(half == 0)
         def _():
+            for chunk in all_chunks[1:]:
+                sideways("a1", a1, 0, chunk).start()
             for chunk in sym_first[1:]:
                 sideways("j1", s1, 1, chunk).wait_recv()
                 start_beside("s1", s1, 1, (chunk,))
-            start_across("a1", a1, 0, all_chunks[1:])
+            start_across("a1", a1, 0, all_chunks)
 
         @pl.when(half == 1)
         def _():
+            sideways("a1", a1, 1, 0, cross_peer).wait_send()
+            for chunk in sym_first[1:]:
+                sideways("j1", s1, 1, chunk).start()
+                sideways("j1", s1, 1, chunk).wait_send()
             for chunk in all_chunks[1:]:
-                sideways("j1", s1, 1, sym_first[1]).wait_send()
                 sideways("a1", a1, 1, chunk, cross_peer).start()
-            for chunk in all_chunks:
-                sideways("a1", a1, 0, chunk).wait_recv()
-                start_across("a1", a1, 0, (chunk,))
 
         gather_sym("s1", s1, 1)
         for kind, at, tag in ((0, core_peer, "c"), (1, side_peer, "x"), (0, cross_peer, "d")):
@@ -354,19 +396,20 @@
                     sideways("j1", s1, 2, chunk).wait_recv()
 
         def put_info(cols, value):
-            j_out[:, cols] = value
-
-        def send_info():
-            copy("jo", j_out, j_out, core_peer).start()
+            inner[:, cols] = value
+            start_result("jo", inner, j_out, cols)
+
+        def put_move(cols, value):
+            anchor[:, cols] = value.astype(BF16)
+            start_result("ao", anchor, a_out, cols)
 
         fresh = early_part(
             "a1", s1.at[0], s1.at[1], a1, v1, lambda cols: s1[2, :, wide(cols)],
-            late_info, put_info, send_info, into(a_out),
+            late_info, put_info, lambda: None, put_move,
         )
-        copy("ao", a_out, a_out, core_peer).start()
         vec_out[1] = fresh
         copy("eo", vec_out.at[1], vec_out.at[1], core_peer).start()
-        copy("co", c_out, c_out, core_peer).wait_recv()
+        end_arrivals("co", weighted, c_out)
         copy("bo", vec_out.at[0], vec_out.at[0], core_peer).wait_recv()
         for step in steps:
             for chunk in all_chunks:
@@ -382,14 +425,15 @@
 
         @pl.when(half == 1)
         def _():
-            for chunk in all_chunks:
+            for chunk in all_chunks[1:]:
                 sideways("a1", a1, 1, chunk, cross_peer).wait_send()
+            for chunk in all_chunks:
                 beside("a1", a1, 1, chunk).wait_send()
 
         for at, tag in vec1_peers:
             vec1(1, at, tag).wait_send()
-        copy("jo", j_out, j_out, core_peer).wait_send()
-        copy("ao", a_out, a_out, core_peer).wait_send()
+        end_results("jo", inner, j_out)
+        end_results("ao", anchor, a_out)
         copy("eo", vec_out.at[1], vec_out.at[1], core_peer).wait_send()
 
     @pl.when(core == 1)
@@ -431,6 +475,10 @@
             for chunk in all_chunks:
                 sideways("c1", s1, 3, chunk).start()
 
+        @pl.when(half == 0)
+        def _():
+            take_move(all_chunks[:1])
+
         gather_sym("s1", s1, 0)
         for kind, at, tag in ((1, core_peer, "c"), (0, side_peer, "x"), (1, cross_peer, "d")):
             vec1(kind, at, tag).wait_recv()
@@ -442,17 +490,17 @@
                     sideways("c1", s1, 3, chunk).wait_recv()
 
         def put_cov(cols, value):
-            c_out[:, cols] = value
+            weighted[:, cols] = value
+            start_result("co", weighted, c_out, cols)
 
         fresh = late_part(
             "a1", s1.at[0], s1.at[1], a1, v1, lambda cols: s1[3, :, wide(cols)],
             late_cov, put_cov
         )
-        copy("co", c_out, c_out, core_peer).start()
         vec_out[0] = fresh
         copy("bo", vec_out.at[0], vec_out.at[0], core_peer).start()
-        copy("jo", j_out, j_out, core_peer).wait_recv()
-        copy("ao", a_out, a_out, core_peer).wait_recv()
+        end_arrivals("jo", inner, j_out)
+        end_arrivals("ao", anchor, a_out)
         copy("eo", vec_out.at[1], vec_out.at[1], core_peer).wait_recv()
         for step in steps:
             for chunk in all_chunks:
@@ -471,7 +519,7 @@
         end_sends("s1", s1, 0)
         for at, tag in vec1_peers:
             vec1(0, at, tag).wait_send()
-        copy("co", c_out, c_out, core_peer).wait_send()
+        end_results("co", weighted, c_out)
         copy("bo", vec_out.at[0], vec_out.at[0], core_peer).wait_send()
 
     end_sends("s0", s0, core)
@@ -503,6 +551,7 @@
     states, width = transition.shape[1:]
     panel = jax.ShapeDtypeStruct((states, width), BF16)
     vmem = pl.BlockSpec(memory_space=pltpu.VMEM)
+    anywhere = pl.BlockSpec(memory_space=pl.ANY)
     square = (states, states)
     count = 48 + 16 * (panels - 1)
     combine = 2 * states * states * width
@@ -510,7 +559,7 @@
         functools.partial(kernel, panels, {}),
         out_shape=(panel, panel, panel, jax.ShapeDtypeStruct((2, 16, states), F32)),
         in_specs=[vmem] * 7,
-        out_specs=(vmem,) * 4,
+        out_specs=(anywhere,) * 3 + (vmem,),
         scratch_shapes=[
             pltpu.VMEM((2,) + square, BF16),
             pltpu.VMEM((2,) + square, BF16),
@@ -524,6 +573,7 @@
             pltpu.VMEM((states, width), BF16),
             pltpu.SemaphoreType.DMA((count,)),
             pltpu.SemaphoreType.DMA((count,)),
+            pltpu.SemaphoreType.DMA((count,)),
         ],
         compiler_params=pltpu.CompilerParams(
             collective_id=0, has_side_effects=True, vmem_limit_bytes=56 * 2**20
@@ -534,7 +584,6 @@
     )(
         transition[0], spread[0], precision[0], drift, belief, probe_hosts, probe_values
     )
-    anywhere = pl.BlockSpec(memory_space=pl.ANY)
     row = jax.ShapeDtypeStruct((1, states), BF16)
     a, b, c, eta, j = pl.pallas_call(
         place,

time: 95.8 us -> 101 us (1.054)
  Pallas kernels: 94.8 us -> 100 us
    pallas_call x1, Pallas kernels: 90.5 us -> 95.9 us  [local(): pl.pallas_call(functools.partial(kernel, panels, {}), out_shape=(panel, p...]
where the time goes in v3:
time: 101 us
  Pallas kernels  100 us (99%)
    pallas_call x1, Pallas kernels, local(): pl.pallas_call(functools.partial(kernel, panels, {}), out_shape=(panel, p...  95.9 us
    pallas_call x1, Pallas kernels, local(): pl.pallas_call(place, out_shape=(panel, row, panel, row, panel), in_specs...  4.3 us

profile of v3, /device:TPU:0, one launch (start us, length us, event | category | flops | bytes accessed | tf_op | source)
XLA Modules:
  0.0 101.0 jit_solution(2120010369924210704)
XLA Ops:
  0.6 95.9 %shard_map.110 = (bf16[1024,512]{1,0:T(8,128)(2,1)}, bf16[1024,512]{1,0:T(8,128)(2,1)}, bf16[1024,512]{1,0:T(8,128)(2,1)}, f32[2,16,1024]{2,1,0:T(8,128)}) custom-call(bf16[1024,512]{1,0:T(8,128)(2,1)} %bitcast.6, bf16[1024,512]{1,0:T(8,128)(2,1)} %bitcast.7, bf16[1024,512]{1,0:T(8,128)(2,1)} %bitcast.8, bf16[1,1024]{1,0:T(2,128)(2,1)} %b_ref.1, ...), custom_call_target="tpu_custom_call" | custom-call | flops 19327352832 | bytes 6291456 | tf_op jit(solution)/shard_map/pallas_call | solution.py:558
  96.6 4.3 %shard_map.111 = (bf16[1024,512]{1,0:T(8,128)(2,1)}, bf16[1,1024]{1,0:T(2,128)(2,1)}, bf16[1024,512]{1,0:T(8,128)(2,1)}, bf16[1,1024]{1,0:T(2,128)(2,1)}, bf16[1024,512]{1,0:T(8,128)(2,1)}) custom-call(bf16[1024,512]{1,0:T(8,128)(2,1)} %get-tuple-element.14.a_ref, bf16[1024,512]{1,0:T(8,128)(2,1)} %get-tuple-element.15.c_ref, ...), custom_call_target="tpu_custom_call" | custom-call | bytes 6291456 | tf_op jit(solution)/shard_map/pallas_call | solution.py:588

commit v4 on v3

--- a/solution.py
+++ b/solution.py
@@ -25,7 +25,7 @@
     panels, names,
     a_ref, c_ref, j_ref, b_ref, eta_ref, hosts_ref, values_ref,
     a_out, c_out, j_out, vec_out,
-    s0, a0, s1, a1, v0, v1, anchor, cur, inner, weighted, send_sem, recv_sem, place_sem,
+    s0, a0, s1, a1, p0, p1, v0, v1, anchor, cur, inner, weighted, send_sem, recv_sem, place_sem,
 ):
     states, width = a_ref.shape
     tile = min(width, 256)
@@ -95,22 +95,38 @@
             ref[:, cols] = value.astype(BF16)
         return put
 
-    def series(cov, info):
+    strip = states // 4
+    strips = 2
+
+    def half_product(name, both, index):
+        cols = pl.ds(pl.multiple_of(core * (strips * strip) + index * strip, strip), strip)
+        return cols, copy(f"{name}p{index}", both.at[:, cols], both.at[:, cols], core_peer)
+
+    def form_both(name, cov, info, both):
+        for index in range(strips):
+            cols, send = half_product(name, both, index)
+            both[:, cols] = dot(cov[...], info[:, cols]).astype(BF16)
+            send.start()
+        for index in range(strips):
+            half_product(name, both, index)[1].wait_recv()
+
+    def end_both(name, both):
+        for index in range(strips):
+            half_product(name, both, index)[1].wait_send()
+
+    def series(both):
         cur[...] = anchor[...]
 
         @pl.loop(0, TERMS)
         def _(repeat):
-            products(info, lambda cols: cur[:, cols], NN, into(inner))
-
             def put(cols, value):
                 cur[:, cols] = (anchor[:, cols].astype(F32) - value).astype(BF16)
 
-            products(cov, lambda cols: inner[:, cols], NN, put)
-
-    def vec_series(start, first, second):
+            products(both, lambda cols: cur[:, cols], NN, put)
+
+    def vec_series(start, both, dims):
         def step(repeat, vector):
-            middle = dot(vector.astype(BF16), first[...])
-            return start - dot(middle.astype(BF16), second[...])
+            return start - dot(vector.astype(BF16), both[...], dims)
 
         return lax.fori_loop(0, TERMS, step, start)
 
@@ -215,9 +231,10 @@
     for step in steps:
         for chunk in sym_chunks:
             across("s0", s0, core, step, chunk).wait_send()
-    start_across("a0", a0, core, all_chunks[:1])
+    start_across("a0", a0, core, all_chunks)
     pass_sym("s0", s0, core)
     gather_sym("s0", s0, core)
+    form_both("p0", s0.at[0], s0.at[1], p0)
     vec0().wait_recv()
 
     def vec1(kind, at, tag):
@@ -232,9 +249,9 @@
             start_across("a1", a1, 1, (chunk,))
             beside("b1", a1, 1, chunk).start()
 
-    def late_part(name, cov, info, moves, vecs, addend, ready, store):
+    def late_part(name, cov, both, moves, vecs, addend, ready, store):
         start = vecs[0, 0] + dot(vecs[1, 1].astype(BF16), cov[...])
-        forward = vec_series(start, info, cov)
+        forward = vec_series(start, both, NT)
         if name == "a1":
             @pl.when(half == 0)
             def _():
@@ -242,8 +259,6 @@
 
         for step in steps:
             across(name, moves, 1, step, 0).wait_recv()
-        if name == "a0":
-            start_across("a0", a0, 1, all_chunks[1:])
         for step in steps:
             onward(name, moves, 1, step, 0).start()
         own_rows = me * width
@@ -252,7 +267,7 @@
             return moves[1, pl.ds(pl.multiple_of(own_rows + cols.start, tile), tile), :]
 
         products(cov, rows, NT, into(anchor))
-        series(cov, info)
+        series(both)
         for step in steps:
             for chunk in all_chunks[1:]:
                 across(name, moves, 1, step, chunk).wait_recv()
@@ -267,27 +282,15 @@
         fresh = dot(forward.astype(BF16), moves[1], NT) + vecs[1, 0]
         return fresh.astype(BF16).astype(F32)
 
-    def early_part(name, cov, info, moves, vecs, addend, ready_info, store_info, sent_info, store_move):
+    def early_part(name, info, both, moves, vecs, addend, ready_info, store_info, sent_info, store_move):
         def vector():
             start = vecs[1, 1] - dot(vecs[0, 0].astype(BF16), info[...])
-            return vec_series(start, cov, info)
-
-        if name == "a1":
-            backward = vector()
-
-            @pl.when(half == 1)
-            def _():
-                for chunk in all_chunks:
-                    sideways("a1", a1, 0, chunk).wait_recv()
-                    start_across("a1", a1, 0, (chunk,))
+            return vec_series(start, both, NN)
 
         anchor[...] = moves[0, :, own_cols]
-        series(cov, info)
-        if name == "a0":
-            start_across("a0", a0, 0, all_chunks[1:])
+        series(both)
         products(info, lambda cols: cur[:, cols], NN, into(weighted))
-        if name == "a0":
-            backward = vector()
+        backward = vector()
         for step in steps:
             for chunk in all_chunks:
                 across(name, moves, 0, step, chunk).wait_recv()
@@ -342,45 +345,48 @@
                 start_beside("s1", s1, 1)
 
         fresh = early_part(
-            "a0", s0.at[0], s0.at[1], a0, v0, lambda cols: j_ref[:, cols],
+            "a0", s0.at[1], p0, a0, v0, lambda cols: j_ref[:, cols],
             lambda: None, store_info, sent_info, store_move,
         )
         share_vec(1, fresh)
 
         @pl.when(half == 0)
         def _():
+            for chunk in all_chunks:
+                sideways("a1", a1, 0, chunk).start()
+            start_across("a1", a1, 0, all_chunks[:1])
             sideways("j1", s1, 1, sym_first[0]).wait_recv()
             start_across("s1", s1, 1, sym_chunks)
             start_beside("s1", s1, 1, sym_first[:1])
-            sideways("a1", a1, 0, 0).start()
 
         @pl.when(half == 1)
         def _():
             start_beside("a1", a1, 1, all_chunks)
             sideways("j1", s1, 1, sym_first[0]).wait_send()
+            for chunk in sym_first[1:]:
+                sideways("j1", s1, 1, chunk).start()
             sideways("a1", a1, 1, 0, cross_peer).start()
 
         pass_sym("s1", s1, 1)
 
         @pl.when(half == 0)
         def _():
-            for chunk in all_chunks[1:]:
-                sideways("a1", a1, 0, chunk).start()
             for chunk in sym_first[1:]:
                 sideways("j1", s1, 1, chunk).wait_recv()
                 start_beside("s1", s1, 1, (chunk,))
-            start_across("a1", a1, 0, all_chunks)
+            start_across("a1", a1, 0, all_chunks[1:])
 
         @pl.when(half == 1)
         def _():
-            sideways("a1", a1, 1, 0, cross_peer).wait_send()
-            for chunk in sym_first[1:]:
-                sideways("j1", s1, 1, chunk).start()
-                sideways("j1", s1, 1, chunk).wait_send()
             for chunk in all_chunks[1:]:
+                sideways("j1", s1, 1, sym_first[1]).wait_send()
                 sideways("a1", a1, 1, chunk, cross_peer).start()
+            for chunk in all_chunks:
+                sideways("a1", a1, 0, chunk).wait_recv()
+                start_across("a1", a1, 0, (chunk,))
 
         gather_sym("s1", s1, 1)
+        form_both("p1", s1.at[0], s1.at[1], p1)
         for kind, at, tag in ((0, core_peer, "c"), (1, side_peer, "x"), (0, cross_peer, "d")):
             vec1(kind, at, tag).wait_recv()
 
@@ -404,7 +410,7 @@
             start_result("ao", anchor, a_out, cols)
 
         fresh = early_part(
-            "a1", s1.at[0], s1.at[1], a1, v1, lambda cols: s1[2, :, wide(cols)],
+            "a1", s1.at[1], p1, a1, v1, lambda cols: s1[2, :, wide(cols)],
             late_info, put_info, lambda: None, put_move,
         )
         vec_out[1] = fresh
@@ -425,9 +431,8 @@
 
         @pl.when(half == 1)
         def _():
-            for chunk in all_chunks[1:]:
+            for chunk in all_chunks:
                 sideways("a1", a1, 1, chunk, cross_peer).wait_send()
-            for chunk in all_chunks:
                 beside("a1", a1, 1, chunk).wait_send()
 
         for at, tag in vec1_peers:
@@ -442,7 +447,7 @@
             s1[cov_slot, :, wide(cols)] = value
 
         fresh = late_part(
-            "a0", s0.at[0], s0.at[1], a0, v0, lambda cols: c_ref[:, cols],
+            "a0", s0.at[0], p0, a0, v0, lambda cols: c_ref[:, cols],
             lambda: None, store_cov
         )
 
@@ -480,6 +485,7 @@
             take_move(all_chunks[:1])
 
         gather_sym("s1", s1, 0)
+        form_both("p1", s1.at[0], s1.at[1], p1)
         for kind, at, tag in ((1, core_peer, "c"), (0, side_peer, "x"), (1, cross_peer, "d")):
             vec1(kind, at, tag).wait_recv()
 
@@ -494,7 +500,7 @@
             start_result("co", weighted, c_out, cols)
 
         fresh = late_part(
-            "a1", s1.at[0], s1.at[1], a1, v1, lambda cols: s1[3, :, wide(cols)],
+            "a1", s1.at[0], p1, a1, v1, lambda cols: s1[3, :, wide(cols)],
             late_cov, put_cov
         )
         vec_out[0] = fresh
@@ -522,6 +528,8 @@
         end_results("co", weighted, c_out)
         copy("bo", vec_out.at[0], vec_out.at[0], core_peer).wait_send()
 
+    end_both("p0", p0)
+    end_both("p1", p1)
     end_sends("s0", s0, core)
     vec0().wait_send()
 
@@ -565,6 +573,8 @@
             pltpu.VMEM((2,) + square, BF16),
             pltpu.VMEM((4,) + square, BF16),
             pltpu.VMEM((2,) + square, BF16),
+            pltpu.VMEM(square, BF16),
+            pltpu.VMEM(square, BF16),
             pltpu.VMEM((2, 2, 16, states), F32),
             pltpu.VMEM((2, 2, 16, states), F32),
             pltpu.VMEM((states, width), BF16),

time: 101 us -> 94.4 us (0.935); the launches traced: 101 us -> 93.1 us
  Pallas kernels: 100 us -> 92.3 us
    pallas_call x1, Pallas kernels: 95.9 us -> 88 us  [local(): pl.pallas_call(functools.partial(kernel, panels, {}), out_shape=(panel, p...]
where the time goes in v4:
time: 94.4 us; the launch traced here: 93.1 us
  Pallas kernels  92.3 us (98%)
    pallas_call x1, Pallas kernels, local(): pl.pallas_call(functools.partial(kernel, panels, {}), out_shape=(panel, p...  88 us
    pallas_call x1, Pallas kernels, local(): pl.pallas_call(place, out_shape=(panel, row, panel, row, panel), in_specs...  4.3 us

profile of v4, /device:TPU:0, one launch (start us, length us, event | category | flops | bytes accessed | tf_op | source)
XLA Modules:
  0.0 93.1 jit_solution(17814466042609815110)
XLA Ops:
  0.6 88.0 %shard_map.110 = (bf16[1024,512]{1,0:T(8,128)(2,1)}, bf16[1024,512]{1,0:T(8,128)(2,1)}, bf16[1024,512]{1,0:T(8,128)(2,1)}, f32[2,16,1024]{2,1,0:T(8,128)}) custom-call(bf16[1024,512]{1,0:T(8,128)(2,1)} %bitcast.6, bf16[1024,512]{1,0:T(8,128)(2,1)} %bitcast.7, bf16[1024,512]{1,0:T(8,128)(2,1)} %bitcast.8, bf16[1,1024]{1,0:T(2,128)(2,1)} %b_ref.1, ...), custom_call_target="tpu_custom_call" | custom-call | flops 19327352832 | bytes 6291456 | tf_op jit(solution)/shard_map/pallas_call | solution.py:566
  88.6 4.3 %shard_map.111 = (bf16[1024,512]{1,0:T(8,128)(2,1)}, bf16[1,1024]{1,0:T(2,128)(2,1)}, bf16[1024,512]{1,0:T(8,128)(2,1)}, bf16[1,1024]{1,0:T(2,128)(2,1)}, bf16[1024,512]{1,0:T(8,128)(2,1)}) custom-call(bf16[1024,512]{1,0:T(8,128)(2,1)} %get-tuple-element.14.a_ref, bf16[1024,512]{1,0:T(8,128)(2,1)} %get-tuple-element.15.c_ref, ...), custom_call_target="tpu_custom_call" | custom-call | bytes 6291456 | tf_op jit(solution)/shard_map/pallas_call | solution.py:598

commit v5 on v3

--- a/solution.py
+++ b/solution.py
@@ -198,6 +198,7 @@
 
     @pl.when(core == 1)
     def _():
+        start_across("a0", a0, 1, all_chunks[:1])
         start_beside("a0", a0, 1, all_chunks)
 
     hosts = jnp.broadcast_to(hosts_ref[...].astype(F32) * 2.0, (8, hosts_ref.shape[1])).T[:, :1]
@@ -215,7 +216,15 @@
     for step in steps:
         for chunk in sym_chunks:
             across("s0", s0, core, step, chunk).wait_send()
-    start_across("a0", a0, core, all_chunks[:1])
+
+    @pl.when(core == 0)
+    def _():
+        start_across("a0", a0, 0, all_chunks)
+
+    @pl.when(core == 1)
+    def _():
+        start_across("a0", a0, 1, all_chunks[1:])
+
     pass_sym("s0", s0, core)
     gather_sym("s0", s0, core)
     vec0().wait_recv()
@@ -242,8 +251,6 @@
 
         for step in steps:
             across(name, moves, 1, step, 0).wait_recv()
-        if name == "a0":
-            start_across("a0", a0, 1, all_chunks[1:])
         for step in steps:
             onward(name, moves, 1, step, 0).start()
         own_rows = me * width
@@ -272,22 +279,10 @@
             start = vecs[1, 1] - dot(vecs[0, 0].astype(BF16), info[...])
             return vec_series(start, cov, info)
 
-        if name == "a1":
-            backward = vector()
-
-            @pl.when(half == 1)
-            def _():
-                for chunk in all_chunks:
-                    sideways("a1", a1, 0, chunk).wait_recv()
-                    start_across("a1", a1, 0, (chunk,))
-
         anchor[...] = moves[0, :, own_cols]
         series(cov, info)
-        if name == "a0":
-            start_across("a0", a0, 0, all_chunks[1:])
         products(info, lambda cols: cur[:, cols], NN, into(weighted))
-        if name == "a0":
-            backward = vector()
+        backward = vector()
         for step in steps:
             for chunk in all_chunks:
                 across(name, moves, 0, step, chunk).wait_recv()
@@ -349,36 +344,38 @@
 
         @pl.when(half == 0)
         def _():
+            for chunk in all_chunks:
+                sideways("a1", a1, 0, chunk).start()
+            start_across("a1", a1, 0, all_chunks[:1])
             sideways("j1", s1, 1, sym_first[0]).wait_recv()
             start_across("s1", s1, 1, sym_chunks)
             start_beside("s1", s1, 1, sym_first[:1])
-            sideways("a1", a1, 0, 0).start()
 
         @pl.when(half == 1)
         def _():
             start_beside("a1", a1, 1, all_chunks)
             sideways("j1", s1, 1, sym_first[0]).wait_send()
+            for chunk in sym_first[1:]:
+                sideways("j1", s1, 1, chunk).start()
             sideways("a1", a1, 1, 0, cross_peer).start()
 
         pass_sym("s1", s1, 1)
 
         @pl.when(half == 0)
         def _():
-            for chunk in all_chunks[1:]:
-                sideways("a1", a1, 0, chunk).start()
             for chunk in sym_first[1:]:
                 sideways("j1", s1, 1, chunk).wait_recv()
                 start_beside("s1", s1, 1, (chunk,))
-            start_across("a1", a1, 0, all_chunks)
+            start_across("a1", a1, 0, all_chunks[1:])
 
         @pl.when(half == 1)
         def _():
-            sideways("a1", a1, 1, 0, cross_peer).wait_send()
-            for chunk in sym_first[1:]:
-                sideways("j1", s1, 1, chunk).start()
-                sideways("j1", s1, 1, chunk).wait_send()
             for chunk in all_chunks[1:]:
+                sideways("j1", s1, 1, sym_first[1]).wait_send()
                 sideways("a1", a1, 1, chunk, cross_peer).start()
+            for chunk in all_chunks:
+                sideways("a1", a1, 0, chunk).wait_recv()
+                start_across("a1", a1, 0, (chunk,))
 
         gather_sym("s1", s1, 1)
         for kind, at, tag in ((0, core_peer, "c"), (1, side_peer, "x"), (0, cross_peer, "d")):
@@ -425,9 +422,8 @@
 
         @pl.when(half == 1)
         def _():
-            for chunk in all_chunks[1:]:
+            for chunk in all_chunks:
                 sideways("a1", a1, 1, chunk, cross_peer).wait_send()
-            for chunk in all_chunks:
                 beside("a1", a1, 1, chunk).wait_send()
 
         for at, tag in vec1_peers:

time: 101 us -> 95.3 us (0.944)
  Pallas kernels: 100 us -> 94.3 us
    pallas_call x1, Pallas kernels: 95.9 us -> 90 us  [local(): pl.pallas_call(functools.partial(kernel, panels, {}), out_shape=(panel, p...]
where the time goes in v5:
time: 95.3 us; the launch traced here: 95.1 us
  Pallas kernels  94.3 us (99%)
    pallas_call x1, Pallas kernels, local(): pl.pallas_call(functools.partial(kernel, panels, {}), out_shape=(panel, p...  90 us
    pallas_call x1, Pallas kernels, local(): pl.pallas_call(place, out_shape=(panel, row, panel, row, panel), in_specs...  4.3 us

profile of v5, /device:TPU:0, one launch (start us, length us, event | category | flops | bytes accessed | tf_op | source)
XLA Modules:
  0.0 95.1 jit_solution(15813103369464251175)
XLA Ops:
  0.6 90.0 %shard_map.110 = (bf16[1024,512]{1,0:T(8,128)(2,1)}, bf16[1024,512]{1,0:T(8,128)(2,1)}, bf16[1024,512]{1,0:T(8,128)(2,1)}, f32[2,16,1024]{2,1,0:T(8,128)}) custom-call(bf16[1024,512]{1,0:T(8,128)(2,1)} %bitcast.6, bf16[1024,512]{1,0:T(8,128)(2,1)} %bitcast.7, bf16[1024,512]{1,0:T(8,128)(2,1)} %bitcast.8, bf16[1,1024]{1,0:T(2,128)(2,1)} %b_ref.1, ...), custom_call_target="tpu_custom_call" | custom-call | flops 19327352832 | bytes 6291456 | tf_op jit(solution)/shard_map/pallas_call | solution.py:554
  90.7 4.3 %shard_map.111 = (bf16[1024,512]{1,0:T(8,128)(2,1)}, bf16[1,1024]{1,0:T(2,128)(2,1)}, bf16[1024,512]{1,0:T(8,128)(2,1)}, bf16[1,1024]{1,0:T(2,128)(2,1)}, bf16[1024,512]{1,0:T(8,128)(2,1)}) custom-call(bf16[1024,512]{1,0:T(8,128)(2,1)} %get-tuple-element.14.a_ref, bf16[1024,512]{1,0:T(8,128)(2,1)} %get-tuple-element.15.c_ref, ...), custom_call_target="tpu_custom_call" | custom-call | bytes 6291456 | tf_op jit(solution)/shard_map/pallas_call | solution.py:584
